TPU v7x, 32 devices: a whole 2x2x4 slice. The times are simulated.
32 devices in a mesh: dom: 4 (over z), rows: 8 (over y, x, core).
Axes of the slice: x: 2, y: 2, z: 4, core: 2. Of those that a mesh axis runs over, the one named last changes fastest.
Arguments:
- blocks: bfloat16 [512, 6, 128, 128], P('rows'), may hold values from -0.15625 to 0.15625
- columns: int32 [512, 6], P('rows'), may hold values from 0 to 511, as said below
- counts: int32 [8], P('rows'), may hold values from 2 to 64, as said below
- start_block: float32 [512, 2, 32, 128], P('rows'), may hold values from -6 to 6
- shift_radius: float32 [8], P('dom'), parts along dimension 0, may hold values from 1 to 1.25
- shift_angle: float32 [8], P('dom'), parts along dimension 0, may hold values from -3.140625 to 3.140625
Outputs:
- solution: float32 [2048, 2, 64, 128], P(('dom', 'rows')), parts along dimension 0
There are 4 independent parts, one for each index of `dom`. A program takes and returns all parts, laid end to end along the dimension named above; an argument that names none is the same for every part. Nothing has to cross between parts.
Inputs may be any that keep to these rules, and one draw needn't show every extreme that they name: `counts`: live block-rows of each device; some device has all 64 live. `columns`: A live block-row i of device d lists first i itself, then three live block-rows of d, then two block-rows among the first 2 of devices other than d. A dead block-row lists only itself.
All inputs are finite; a program needn't handle non-finite values.
Results may differ from a plain program's by a relative error of at most 0.0038.
Values may be sent and summed in bfloat16 or wider, within the bound.
A program may use at most 128 MiB of HBM per device.

v0:
```python
import functools

import jax
import jax.numpy as jnp
from jax import lax
from jax.experimental import pallas as pl
from jax.experimental.pallas import tpu as pltpu
from jax.sharding import PartitionSpec as P

HB = 2
ITERS = 4
NEAR = 4
F32 = jnp.float32
BF16 = jnp.bfloat16


def pick_unroll(total, want):
    while total % want:
        want -= 1
    return want


def pair_counts(slots, far, n):
    far_rows = (n - 1) * HB
    far_pairs = (slots * far + far_rows) // 2
    near_pairs = (slots * NEAR + slots) // 2
    return -(-far_pairs // 8) * 8, -(-near_pairs // 8) * 8


def split(entry, width):
    if width & (width - 1):
        k = lax.div(entry, jnp.int32(width))
        return k, entry - k * width
    shift = width.bit_length() - 1
    return lax.shift_right_logical(entry, jnp.int32(shift)), entry & (width - 1)


def kernel(
    n, slots, far, nvec, shifts,
    meta, radius, angle, blocks, start, out,
    near_w, far_w, turned, weight, drive, upper, lower, near_sum, far_sum,
    pair_out, pair_in, send_terms, heads, far_heads, terms,
    load_sem, far_sem, near_sem, head_send, head_recv, pass_send, pass_recv,
    pair_send, pair_recv, term_send, term_recv,
):
    me = lax.axis_index("rows")
    near_total = slots * (NEAR - 1)
    far_total = slots * far
    far_rows = (n - 1) * HB
    far_pairs, near_pairs = pair_counts(slots, far, n)
    chips = n // 2
    core = lax.rem(me, 2)
    chip = me // 2

    def partner(off):
        if off == 0:
            return chip * 2 + 1 - core
        return lax.rem(chip + off, chips) * 2 + core

    at_keep = 2 * (far_pairs + near_pairs)
    at_far_last = at_keep + far_pairs + near_pairs
    at_near_last = at_far_last + far_rows
    at_near_col = at_near_last + slots
    at_far_col = at_near_col + near_total
    at_count = at_far_col + far_total

    load_start = pltpu.make_async_copy(start, drive, load_sem.at[0])
    chunk = pick_unroll(slots, 8)
    width = turned.shape[2]

    def load_far(i):
        rows = pl.ds(i * chunk, chunk)
        return pltpu.make_async_copy(blocks.at[rows, NEAR:], far_w.at[rows], far_sem.at[i])

    def load_near(i):
        rows = pl.ds(i * chunk, chunk)
        return pltpu.make_async_copy(blocks.at[rows, :NEAR], near_w.at[rows], near_sem.at[i])

    load_start.start()
    for i in range(slots // chunk):
        load_far(i).start()
        load_near(i).start()

    barrier = pltpu.get_barrier_semaphore()
    for off in range(chips):
        pl.semaphore_signal(
            barrier, inc=1, device_id={"rows": partner(off)},
            device_id_type=pl.DeviceIdType.MESH,
        )

    def rotated(values):
        pieces = []
        for s in range(shifts):
            re = values[(2 * s) * nvec:(2 * s + 1) * nvec]
            im = values[(2 * s + 1) * nvec:(2 * s + 2) * nvec]
            w_re = weight[s]
            w_im = weight[shifts + s]
            pieces.append(w_re * re - w_im * im)
            pieces.append(w_re * im + w_im * re)
        return jnp.concatenate(pieces, 0)

    def driven(k, half):
        return jnp.concatenate([drive[k, half]] * shifts, 0)

    for s in range(shifts):
        turn_by = jnp.full(weight.shape[1:], angle[s], F32)
        size = jnp.full(weight.shape[1:], radius[s], F32)
        weight[s] = jnp.cos(turn_by) / size
        weight[shifts + s] = -jnp.sin(turn_by) / size
    load_start.wait()

    def begin(k, carry):
        alive = (k < meta[at_count]).astype(F32)
        drive[k] = drive[k] * alive
        upper[0, k] = rotated(driven(k, 0)).astype(BF16)
        lower[0, k] = rotated(driven(k, 1)).astype(BF16)
        return carry

    lax.fori_loop(0, slots, begin, 0, unroll=2)
    for p in range(2):
        upper[p, slots] = jnp.zeros(upper.shape[2:], upper.dtype)
    near_w[slots, 0] = jnp.zeros(near_w.shape[2:], near_w.dtype)
    far_w[slots, 0] = jnp.zeros(far_w.shape[2:], far_w.dtype)
    near_sum[0] = jnp.zeros(near_sum.shape[1:], near_sum.dtype)
    far_sum[0] = jnp.zeros(far_sum.shape[1:], far_sum.dtype)
    pl.semaphore_wait(barrier, chips)

    def send(source, target, send_sem, recv_sem, off):
        return pltpu.make_async_remote_copy(
            src_ref=source, dst_ref=target, send_sem=send_sem, recv_sem=recv_sem,
            device_id={"rows": partner(off)}, device_id_type=pl.DeviceIdType.MESH,
        )

    def head_copy(p, off):
        there = 0 if off == 0 else 2 * (chips - off) - 1
        return send(
            lower.at[p, pl.ds(0, HB)], heads.at[p, pl.ds(there * HB, HB)],
            head_send.at[off], head_recv.at[p, 0 if off == 0 else chips - off], off,
        )

    def pass_copy(p, off):
        return send(
            heads.at[p, pl.ds((2 * off - 1) * HB, HB)], heads.at[p, pl.ds(2 * off * HB, HB)],
            pass_send.at[off - 1], pass_recv.at[p, off - 1], 0,
        )

    def pair_copy(p):
        return send(pair_out, pair_in.at[p], pair_send.at[0], pair_recv.at[p], 0)

    def term_copy(p, off):
        return send(
            send_terms.at[pl.ds((off - 1) * HB, HB)],
            terms.at[p, pl.ds((chips - off - 1) * HB, HB)],
            term_send.at[off - 1], term_recv.at[p, chips - off - 1], off,
        )

    def dot(a, b):
        return jnp.dot(a, b, preferred_element_type=F32)

    def sweep(s, last):
        p = lax.rem(s, 2)
        q = 1 - p
        for off in range(1, chips):
            head_copy(p, off).start()
        head_copy(p, 0).start()

        zero = jnp.zeros(upper.shape[2:], F32)

        def running(first, low, high, acc, blocks_of, weights, sums):
            step = pick_unroll(high - low, 40)
            group = pick_unroll(step, 8)

            def go(i, acc):
                for g in range(step // group):
                    found = []
                    for u in range(group):
                        j = low + i * step + g * group + u
                        lhs, rhs = [], []
                        for side in range(2):
                            e = meta[2 * (first + j) + side]
                            k, c = split(e, blocks_of)
                            lhs.append(upper[p, k])
                            rhs.append(weights[k, c])
                        found.append(dot(jnp.concatenate(lhs, 1), jnp.concatenate(rhs, 0)))
                    for u in range(group):
                        j = low + i * step + g * group + u
                        acc = acc * meta[at_keep + first + j].astype(F32) + found[u]
                        sums[j + 1] = acc.astype(sums.dtype)
                return acc

            return lax.fori_loop(0, (high - low) // step, go, acc)

        running(0, 0, far_pairs, zero, far, far_w, far_sum)
        for off in range(chips):
            for h in range(HB):
                row = 2 * off * HB + h
                pair_out[off * HB + h] = far_sum[meta[at_far_last + row]]
        pair_copy(p).start()
        half = near_pairs // 2
        acc = running(far_pairs, 0, half, zero, NEAR, near_w, near_sum)
        pair_copy(p).wait_recv()
        for off in range(1, chips):
            for h in range(HB):
                row = (2 * off - 1) * HB + h
                send_terms[(off - 1) * HB + h] = (
                    far_sum[meta[at_far_last + row]] + pair_in[p, off * HB + h]
                ).astype(BF16)
            term_copy(p, off).start()
        for off in range(1, chips):
            head_copy(p, chips - off).wait_recv()
            pass_copy(p, off).start()
        running(far_pairs, half, near_pairs, acc, NEAR, near_w, near_sum)

        def bottom(k, extra):
            value = driven(k, 1) + near_sum[meta[at_near_last + k]]
            if extra:
                value = value + pair_in[p, k]
                for off in range(chips - 1):
                    value = value + terms[p, off * HB + k].astype(F32)
            value = rotated(value)
            if last:
                out[k, 1] = value
            else:
                lower[q, k] = value.astype(BF16)

        def bottom_step(k, carry):
            bottom(k, False)
            return carry

        lax.fori_loop(HB, slots, bottom_step, 0, unroll=16)

        head_copy(p, 0).wait_recv()
        for off in range(1, chips):
            pass_copy(p, off).wait_recv()
        for row in range(far_rows):
            far_heads[row] = heads[p, row]

        step_top = pick_unroll(slots, 16)
        group_top = pick_unroll(step_top, 4)

        def top_step(i, carry):
            for g in range(step_top // group_top):
                found = []
                for u in range(group_top):
                    k = i * step_top + g * group_top + u
                    tiles = [lower[p, k]]
                    for c in range(NEAR - 1):
                        tiles.append(lower[p, meta[at_near_col + k * (NEAR - 1) + c]])
                    for c in range(far):
                        tiles.append(far_heads[meta[at_far_col + k * far + c]])
                    found.append(dot(jnp.concatenate(tiles, 1), turned[k]))
                for u in range(group_top):
                    k = i * step_top + g * group_top + u
                    alive = (k < meta[at_count]).astype(F32)
                    value = rotated(driven(k, 0) + found[u] * alive)
                    if last:
                        out[k, 0] = value
                    else:
                        upper[q, k] = value.astype(BF16)
            return carry

        lax.fori_loop(0, slots // step_top, top_step, 0)

        for off in range(1, chips):
            term_copy(p, off).wait_recv()
        for k in range(HB):
            bottom(k, True)
        pair_copy(p).wait_send()
        for off in range(chips):
            head_copy(p, off).wait_send()
        for off in range(1, chips):
            pass_copy(p, off).wait_send()
            term_copy(p, off).wait_send()


    def turn(i, carry):
        load_far(i).wait()
        load_near(i).wait()
        for u in range(chunk):
            k = i * chunk + u
            for c in range(NEAR + far):
                block = near_w[k, c] if c < NEAR else far_w[k, c - NEAR]
                turned[k, c * width:(c + 1) * width] = block.T
        return carry

    lax.fori_loop(0, slots // chunk, turn, 0)

    def middle(s, carry):
        sweep(s, False)
        return carry

    lax.fori_loop(0, ITERS - 1, middle, 0)
    sweep(ITERS - 1, True)


def plan(columns, counts, me, n):
    slots, stored = columns.shape
    far = stored - NEAR
    owner = columns // slots
    within = columns - owner * slots
    chips = n // 2
    rel = 2 * lax.rem(owner // 2 - me // 2 + chips, chips) + lax.rem(owner + me, 2)
    far_rows = (n - 1) * HB
    far_pairs, near_pairs = pair_counts(slots, far, n)
    near_all = within[:, :NEAR].reshape(-1)
    far_col = jnp.clip((rel - 1) * HB + within, 0, far_rows - 1)[:, NEAR:].reshape(-1)
    far_total = far_col.shape[0]
    dest = jnp.concatenate([far_col, far_rows + near_all])
    here = jnp.arange(dest.shape[0], dtype=jnp.int32)
    entry = jnp.where(here < far_total, here, here - far_total)
    rows = jnp.arange(far_rows + slots, dtype=jnp.int32)
    same = dest[None, :] == dest[:, None]
    order = jnp.sum((same & (here[None, :] < here[:, None])).astype(jnp.int32), 1)
    even = 1 - (order & 1)
    is_near = (rows >= far_rows).astype(jnp.int32)
    dest_near = (dest >= far_rows).astype(jnp.int32)
    ahead_rows = is_near * far_pairs + jnp.sum(
        jnp.where((dest[None, :] < rows[:, None]) & (dest_near[None, :] == is_near[:, None]),
                  even[None, :], 0), 1)
    own_rows = jnp.sum(jnp.where(dest[None, :] == rows[:, None], even[None, :], 0), 1)
    ahead = dest_near * far_pairs + jnp.sum(
        jnp.where((dest[None, :] < dest[:, None]) & (dest_near[None, :] == dest_near[:, None]),
                  even[None, :], 0), 1)
    place = 2 * ahead + order
    pairs = far_pairs + near_pairs
    spots = jnp.arange(2 * pairs, dtype=jnp.int32)
    empty = jnp.where(spots < 2 * far_pairs, slots * far, slots * NEAR)
    listed = jnp.sum(
        jnp.where(place[None, :] == spots[:, None], entry[None, :] - empty[:, None], 0), 1
    ) + empty
    pair_ids = jnp.arange(pairs, dtype=jnp.int32)
    starts = (ahead_rows[None, :] == pair_ids[:, None]) & (own_rows[None, :] > 0)
    keep = 1 - jnp.sum(starts.astype(jnp.int32), 1)
    ends = jnp.where(own_rows > 0, ahead_rows + own_rows - is_near * far_pairs, 0)
    return jnp.concatenate(
        [listed, keep, ends, within[:, 1:NEAR].reshape(-1), far_col, counts]
    )


def body(blocks, columns, counts, start_block, shift_radius, shift_angle):
    me = lax.axis_index("rows")
    n = lax.axis_size("rows")
    slots, stored, width = blocks.shape[0], blocks.shape[1], blocks.shape[-1]
    far = stored - NEAR
    shifts = shift_radius.shape[0]
    two_nvec = start_block.shape[2]
    cols = shifts * two_nvec
    meta = plan(columns, counts, me, n)
    chips = n // 2
    far_rows = (n - 1) * HB
    far_pairs, near_pairs = pair_counts(slots, far, n)
    flops = ITERS * 4 * slots * stored * width * width * cols
    smem = pl.BlockSpec(memory_space=pltpu.SMEM)
    hbm = pl.BlockSpec(memory_space=pl.ANY)
    return pl.pallas_call(
        functools.partial(kernel, n, slots, far, two_nvec // 2, shifts),
        out_shape=pltpu.VMEM((slots, 2, cols, width), F32),
        in_specs=[smem, smem, smem, hbm, hbm],
        out_specs=pl.BlockSpec(memory_space=pltpu.VMEM),
        scratch_shapes=[
            pltpu.VMEM((slots + 1, NEAR, width, width), BF16),
            pltpu.VMEM((slots + 1, far, width, width), BF16),
            pltpu.VMEM((slots, stored * width, width), BF16),
            pltpu.VMEM((2 * shifts, two_nvec // 2, width), F32),
            pltpu.VMEM(start_block.shape, F32),
            pltpu.VMEM((2, slots + 1, cols, width), BF16),
            pltpu.VMEM((2, slots, cols, width), BF16),
            pltpu.VMEM((near_pairs + 1, cols, width), F32),
            pltpu.VMEM((far_pairs + 1, cols, width), F32),
            pltpu.VMEM((chips * HB, cols, width), F32),
            pltpu.VMEM((2, chips * HB, cols, width), F32),
            pltpu.VMEM(((chips - 1) * HB, cols, width), BF16),
            pltpu.VMEM((2, far_rows, cols, width), BF16),
            pltpu.VMEM((far_rows, cols, width), BF16),
            pltpu.VMEM((2, (chips - 1) * HB, cols, width), BF16),
            pltpu.SemaphoreType.DMA((1,)),
            pltpu.SemaphoreType.DMA((slots // pick_unroll(slots, 8),)),
            pltpu.SemaphoreType.DMA((slots // pick_unroll(slots, 8),)),
            pltpu.SemaphoreType.DMA((chips,)),
            pltpu.SemaphoreType.DMA((2, chips)),
            pltpu.SemaphoreType.DMA((chips - 1,)),
            pltpu.SemaphoreType.DMA((2, chips - 1)),
            pltpu.SemaphoreType.DMA((1,)),
            pltpu.SemaphoreType.DMA((2,)),
            pltpu.SemaphoreType.DMA((chips - 1,)),
            pltpu.SemaphoreType.DMA((2, chips - 1)),
        ],
        compiler_params=pltpu.CompilerParams(
            collective_id=0, has_side_effects=True, vmem_limit_bytes=54 * 1024 * 1024
        ),
        cost_estimate=pl.CostEstimate(
            flops=flops, bytes_accessed=2 * blocks.size, transcendentals=0
        ),
    )(meta, shift_radius, shift_angle, blocks, start_block)


def solution(mesh):
    placed = (
        P("rows", None, None, None),
        P("rows", None),
        P("rows"),
        P("rows", None, None, None),
        P("dom"),
        P("dom"),
    )
    return jax.shard_map(
        body,
        mesh=mesh,
        in_specs=placed,
        out_specs=P(("dom", "rows"), None, None, None),
        check_vma=False,
    )
```

profile of v0, /device:TPU:0, one launch (start us, length us, event | category | flops | bytes accessed | tf_op | source)
XLA Modules:
  0.0 50.8 jit_solution(5886077079557377262)
XLA Ops:
  0.7 0.7 %multiply_subtract_fusion = (s32[64,6]{0,1:T(8,128)S(1)}, s32[64,6]{0,1:T(8,128)S(1)}) fusion(s32[64,6]{0,1:T(8,128)} %param.7, s32[]{:T(128)S(6)} %axis_index.12, s32[]{:T(128)S(6)} %select_n.52), kind=kLoop, calls=%fused_computation.40 | loop fusion | flops 20352 | bytes 4616 | tf_op jit(solution)/shard_map/sub | solution.py:300
  1.4 0.1 copy.13
  1.5 0.1 reshape.95
  1.7 0.1 copy.12
  1.8 0.1 add.71
  1.9 0.1 copy.11
  2.0 0.1 concatenate.19
  2.1 0.2 convert_reduce_fusion
  2.4 0.2 select_reduce_fusion.2
  2.6 0.3 select_reduce_fusion.1
  2.9 0.3 select_reduce_fusion
  3.2 0.1 convert_reduce_fusion.1
  3.3 0.7 %concatenate.21.meta = s32[1095]{0:T(1024)} concatenate(s32[464]{0:T(512)S(1)} %fusion.18, s32[232]{0:T(256)S(1)} %broadcast_subtract_fusion, s32[78]{0:T(128)S(1)} %get-tuple-element.11, s32[192]{0:T(256)S(1)} %reshape.95, s32[128]{0:T(128)S(1)} %concatenate.19, s32[1]{0:T(128)S(6)} %copy.18), dimensions={0} | concatenate | bytes 8760 | tf_op jit(solution)/shard_map/concatenate | solution.py:335
  4.0 44.8 %shard_map.64 = f32[64,2,64,128]{3,2,1,0:T(8,128)S(1)} custom-call(s32[1095]{0:T(1024)} %concatenate.21.meta, f32[2]{0:T(128)} %radius.1, f32[2]{0:T(128)} %angle.1, bf16[64,6,128,128]{3,2,1,0:T(8,128)(2,1)} %blocks.1, f32[64,2,32,128]{3,2,1,0:T(8,128)} %start.1), custom_call_target="tpu_custom_call" | custom-call | flops 6442450944 | bytes 12582912 | tf_op jit(solution)/shard_map/pallas_call | solution.py:355
  48.8 2.0 %copy.17 = f32[64,2,64,128]{3,2,1,0:T(8,128)} copy(f32[64,2,64,128]{3,2,1,0:T(8,128)S(1)} %shard_map.64) | data formatting | bytes 8388608
  (15 shorter events, 0.1 us)
where the time goes:
time: 51 us; the launch traced here: 50.8 us
  Pallas kernels  44.8 us (88%)
  local copies, waits for them, and re-layouts  3.41 us (7%)
  other arithmetic  1.82 us (4%)
  between operations  0.76 us (1%)
    pallas_call x1, Pallas kernels, body(): pl.pallas_call(functools.partial(kernel, n, slots, far, two_nvec // 2, sh...  44.8 us
    unnamed x2, local copies, waits for them, and re-layouts  2.03 us

commit v1 on v0

--- a/solution.py
+++ b/solution.py
@@ -116,7 +116,7 @@
         lower[0, k] = rotated(driven(k, 1)).astype(BF16)
         return carry
 
-    lax.fori_loop(0, slots, begin, 0, unroll=2)
+    lax.fori_loop(0, slots, begin, 0, unroll=8)
     for p in range(2):
         upper[p, slots] = jnp.zeros(upper.shape[2:], upper.dtype)
     near_w[slots, 0] = jnp.zeros(near_w.shape[2:], near_w.dtype)
@@ -167,7 +167,7 @@
         zero = jnp.zeros(upper.shape[2:], F32)
 
         def running(first, low, high, acc, blocks_of, weights, sums):
-            step = pick_unroll(high - low, 40)
+            step = pick_unroll(high - low, 80)
             group = pick_unroll(step, 8)
 
             def go(i, acc):
@@ -227,7 +227,7 @@
             bottom(k, False)
             return carry
 
-        lax.fori_loop(HB, slots, bottom_step, 0, unroll=16)
+        lax.fori_loop(HB, slots, bottom_step, 0, unroll=pick_unroll(slots - HB, 31))
 
         head_copy(p, 0).wait_recv()
         for off in range(1, chips):
@@ -235,7 +235,7 @@
         for row in range(far_rows):
             far_heads[row] = heads[p, row]
 
-        step_top = pick_unroll(slots, 16)
+        step_top = pick_unroll(slots, 32)
         group_top = pick_unroll(step_top, 4)
 
         def top_step(i, carry):
@@ -291,6 +291,19 @@
 
     lax.fori_loop(0, ITERS - 1, middle, 0)
     sweep(ITERS - 1, True)
+
+
+def store(source, out, sems):
+    parts = sems.shape[0]
+    rows = source.shape[0] // parts
+    copies = []
+    for i in range(parts):
+        part = pl.ds(i * rows, rows)
+        copies.append(pltpu.make_async_copy(source.at[part], out.at[part], sems.at[i]))
+    for copy in copies:
+        copy.start()
+    for copy in copies:
+        copy.wait()
 
 
 def plan(columns, counts, me, n):
@@ -352,7 +365,7 @@
     flops = ITERS * 4 * slots * stored * width * width * cols
     smem = pl.BlockSpec(memory_space=pltpu.SMEM)
     hbm = pl.BlockSpec(memory_space=pl.ANY)
-    return pl.pallas_call(
+    found = pl.pallas_call(
         functools.partial(kernel, n, slots, far, two_nvec // 2, shifts),
         out_shape=pltpu.VMEM((slots, 2, cols, width), F32),
         in_specs=[smem, smem, smem, hbm, hbm],
@@ -392,6 +405,14 @@
             flops=flops, bytes_accessed=2 * blocks.size, transcendentals=0
         ),
     )(meta, shift_radius, shift_angle, blocks, start_block)
+    return pl.pallas_call(
+        store,
+        out_shape=jax.ShapeDtypeStruct(found.shape, F32),
+        in_specs=[pl.BlockSpec(memory_space=pltpu.VMEM)],
+        out_specs=hbm,
+        scratch_shapes=[pltpu.SemaphoreType.DMA((pick_unroll(slots, 8),))],
+        compiler_params=pltpu.CompilerParams(vmem_limit_bytes=8 * 1024 * 1024),
+    )(found)
 
 
 def solution(mesh):

time: 51 us -> 49.3 us (0.967)
  local copies, waits for them, and re-layouts: 3.41 us -> 1.39 us
    pallas_call x0 -> x1, Pallas kernels: none -> 2.07 us  [body(): pl.pallas_call(store, out_shape=jax.ShapeDtypeStruct(found.shape, F32), i...]
    unnamed x2 -> x1, local copies, waits for them, and re-layouts: 2.03 us -> 0.02 us
    pallas_call x1, Pallas kernels: 44.8 us -> 43 us  [body(): pl.pallas_call(functools.partial(kernel, n, slots, far, two_nvec // 2, sh...]
where the time goes in v1:
time: 49.3 us; the launch traced here: 49.1 us
  Pallas kernels  45.1 us (91%)
  other arithmetic  1.82 us (4%)
  local copies, waits for them, and re-layouts  1.39 us (3%)
  between operations  0.76 us (2%)
    pallas_call x1, Pallas kernels, body(): pl.pallas_call(functools.partial(kernel, n, slots, far, two_nvec // 2, sh...  43 us
    pallas_call x1, Pallas kernels, body(): pl.pallas_call(store, out_shape=jax.ShapeDtypeStruct(found.shape, F32), i...  2.07 us

profile of v1, /device:TPU:0, one launch (start us, length us, event | category | flops | bytes accessed | tf_op | source)
XLA Modules:
  0.0 49.1 jit_solution(9263588412986717251)
XLA Ops:
  0.7 0.7 %multiply_subtract_fusion = (s32[64,6]{0,1:T(8,128)S(1)}, s32[64,6]{0,1:T(8,128)S(1)}) fusion(s32[64,6]{0,1:T(8,128)} %param.7, s32[]{:T(128)S(6)} %axis_index.12, s32[]{:T(128)S(6)} %select_n.52), kind=kLoop, calls=%fused_computation.40 | loop fusion | flops 20352 | bytes 4616 | tf_op jit(solution)/shard_map/sub | solution.py:313
  1.4 0.1 copy.13
  1.5 0.1 reshape.95
  1.7 0.1 copy.12
  1.8 0.1 add.71
  1.9 0.1 copy.11
  2.0 0.1 concatenate.19
  2.1 0.2 convert_reduce_fusion
  2.4 0.2 select_reduce_fusion.2
  2.6 0.3 select_reduce_fusion.1
  2.9 0.3 select_reduce_fusion
  3.2 0.1 convert_reduce_fusion.1
  3.3 0.7 %concatenate.21.meta = s32[1095]{0:T(1024)} concatenate(s32[464]{0:T(512)S(1)} %fusion.18, s32[232]{0:T(256)S(1)} %broadcast_subtract_fusion, s32[78]{0:T(128)S(1)} %get-tuple-element.11, s32[192]{0:T(256)S(1)} %reshape.95, s32[128]{0:T(128)S(1)} %concatenate.19, s32[1]{0:T(128)S(6)} %copy.16), dimensions={0} | concatenate | bytes 8760 | tf_op jit(solution)/shard_map/concatenate | solution.py:348
  4.0 43.0 %shard_map.64.source = f32[64,2,64,128]{3,2,1,0:T(8,128)S(1)} custom-call(s32[1095]{0:T(1024)} %concatenate.21.meta, f32[2]{0:T(128)} %radius.1, f32[2]{0:T(128)} %angle.1, bf16[64,6,128,128]{3,2,1,0:T(8,128)(2,1)} %blocks.1, f32[64,2,32,128]{3,2,1,0:T(8,128)} %start.1), custom_call_target="tpu_custom_call" | custom-call | flops 6442450944 | bytes 12582912 | tf_op jit(solution)/shard_map/pallas_call | solution.py:368
  47.0 2.1 %shard_map.65 = f32[64,2,64,128]{3,2,1,0:T(8,128)} custom-call(f32[64,2,64,128]{3,2,1,0:T(8,128)S(1)} %shard_map.64.source), custom_call_target="tpu_custom_call" | custom-call | tf_op jit(solution)/shard_map/pallas_call | solution.py:408
  (15 shorter events, 0.1 us)

commit v2 on v1

--- a/solution.py
+++ b/solution.py
@@ -79,6 +79,7 @@
     load_start.start()
     for i in range(slots // chunk):
         load_far(i).start()
+    for i in range(slots // chunk):
         load_near(i).start()
 
     barrier = pltpu.get_barrier_semaphore()
@@ -157,8 +158,8 @@
     def dot(a, b):
         return jnp.dot(a, b, preferred_element_type=F32)
 
-    def sweep(s, last):
-        p = lax.rem(s, 2)
+    def sweep(s, last, first):
+        p = s % 2 if isinstance(s, int) else lax.rem(s, 2)
         q = 1 - p
         for off in range(1, chips):
             head_copy(p, off).start()
@@ -190,6 +191,9 @@
 
             return lax.fori_loop(0, (high - low) // step, go, acc)
 
+        if first:
+            for i in range(slots // chunk):
+                load_far(i).wait()
         running(0, 0, far_pairs, zero, far, far_w, far_sum)
         for off in range(chips):
             for h in range(HB):
@@ -197,6 +201,9 @@
                 pair_out[off * HB + h] = far_sum[meta[at_far_last + row]]
         pair_copy(p).start()
         half = near_pairs // 2
+        if first:
+            for i in range(slots // chunk):
+                load_near(i).wait()
         acc = running(far_pairs, 0, half, zero, NEAR, near_w, near_sum)
         pair_copy(p).wait_recv()
         for off in range(1, chips):
@@ -235,7 +242,7 @@
         for row in range(far_rows):
             far_heads[row] = heads[p, row]
 
-        step_top = pick_unroll(slots, 32)
+        step_top = pick_unroll(slots, 16 if first else 32)
         group_top = pick_unroll(step_top, 4)
 
         def top_step(i, carry):
@@ -248,6 +255,10 @@
                         tiles.append(lower[p, meta[at_near_col + k * (NEAR - 1) + c]])
                     for c in range(far):
                         tiles.append(far_heads[meta[at_far_col + k * far + c]])
+                    if first:
+                        for c in range(NEAR + far):
+                            block = near_w[k, c] if c < NEAR else far_w[k, c - NEAR]
+                            turned[k, c * width:(c + 1) * width] = block.T
                     found.append(dot(jnp.concatenate(tiles, 1), turned[k]))
                 for u in range(group_top):
                     k = i * step_top + g * group_top + u
@@ -273,24 +284,14 @@
             term_copy(p, off).wait_send()
 
 
-    def turn(i, carry):
-        load_far(i).wait()
-        load_near(i).wait()
-        for u in range(chunk):
-            k = i * chunk + u
-            for c in range(NEAR + far):
-                block = near_w[k, c] if c < NEAR else far_w[k, c - NEAR]
-                turned[k, c * width:(c + 1) * width] = block.T
+    def middle(s, carry):
+        sweep(s, False, False)
         return carry
 
-    lax.fori_loop(0, slots // chunk, turn, 0)
-
-    def middle(s, carry):
-        sweep(s, False)
-        return carry
-
-    lax.fori_loop(0, ITERS - 1, middle, 0)
-    sweep(ITERS - 1, True)
+    sweep(0, ITERS == 1, True)
+    if ITERS > 1:
+        lax.fori_loop(1, ITERS - 1, middle, 0)
+        sweep(ITERS - 1, True, False)
 
 
 def store(source, out, sems):

time: 49.3 us -> 48 us (0.974)
  Pallas kernels: 45.1 us -> 43.9 us
    pallas_call x1, Pallas kernels: 43 us -> 41.8 us  [body(): pl.pallas_call(functools.partial(kernel, n, slots, far, two_nvec // 2, sh...]
where the time goes in v2:
time: 48 us; the launch traced here: 47.8 us
  Pallas kernels  43.9 us (91%)
  other arithmetic  1.82 us (4%)
  local copies, waits for them, and re-layouts  1.39 us (3%)
  between operations  0.76 us (2%)
    pallas_call x1, Pallas kernels, body(): pl.pallas_call(functools.partial(kernel, n, slots, far, two_nvec // 2, sh...  41.8 us
    pallas_call x1, Pallas kernels, body(): pl.pallas_call(store, out_shape=jax.ShapeDtypeStruct(found.shape, F32), i...  2.07 us

profile of v2, /device:TPU:0, one launch (start us, length us, event | category | flops | bytes accessed | tf_op | source)
XLA Modules:
  0.0 47.8 jit_solution(12701508432538731014)
XLA Ops:
  0.7 0.7 %multiply_subtract_fusion = (s32[64,6]{0,1:T(8,128)S(1)}, s32[64,6]{0,1:T(8,128)S(1)}) fusion(s32[64,6]{0,1:T(8,128)} %param.7, s32[]{:T(128)S(6)} %axis_index.12, s32[]{:T(128)S(6)} %select_n.52), kind=kLoop, calls=%fused_computation.40 | loop fusion | flops 20352 | bytes 4616 | tf_op jit(solution)/shard_map/sub | solution.py:314
  1.4 0.1 copy.13
  1.5 0.1 reshape.95
  1.7 0.1 copy.12
  1.8 0.1 add.71
  1.9 0.1 copy.11
  2.0 0.1 concatenate.19
  2.1 0.2 convert_reduce_fusion
  2.4 0.2 select_reduce_fusion.2
  2.6 0.3 select_reduce_fusion.1
  2.9 0.3 select_reduce_fusion
  3.2 0.1 convert_reduce_fusion.1
  3.3 0.7 %concatenate.21.meta = s32[1095]{0:T(1024)} concatenate(s32[464]{0:T(512)S(1)} %fusion.18, s32[232]{0:T(256)S(1)} %broadcast_subtract_fusion, s32[78]{0:T(128)S(1)} %get-tuple-element.11, s32[192]{0:T(256)S(1)} %reshape.95, s32[128]{0:T(128)S(1)} %concatenate.19, s32[1]{0:T(128)S(6)} %copy.16), dimensions={0} | concatenate | bytes 8760 | tf_op jit(solution)/shard_map/concatenate | solution.py:349
  4.0 41.8 %shard_map.64.source = f32[64,2,64,128]{3,2,1,0:T(8,128)S(1)} custom-call(s32[1095]{0:T(1024)} %concatenate.21.meta, f32[2]{0:T(128)} %radius.1, f32[2]{0:T(128)} %angle.1, bf16[64,6,128,128]{3,2,1,0:T(8,128)(2,1)} %blocks.1, f32[64,2,32,128]{3,2,1,0:T(8,128)} %start.1), custom_call_target="tpu_custom_call" | custom-call | flops 6442450944 | bytes 12582912 | tf_op jit(solution)/shard_map/pallas_call | solution.py:369
  45.7 2.1 %shard_map.65 = f32[64,2,64,128]{3,2,1,0:T(8,128)} custom-call(f32[64,2,64,128]{3,2,1,0:T(8,128)S(1)} %shard_map.64.source), custom_call_target="tpu_custom_call" | custom-call | tf_op jit(solution)/shard_map/pallas_call | solution.py:409
  (15 shorter events, 0.1 us)
